TPU v7x, 256 devices: a whole 4x4x8 slice. The times are simulated.
256 devices in a mesh: out: 8 (over z), inp: 32 (over y, x, core).
Axes of the slice: x: 4, y: 4, z: 8, core: 2. Of those that a mesh axis runs over, the one named last changes fastest.
Arguments:
- weight_delta: bfloat16 [8192, 38912], P('inp', 'out'), may hold values from -6 to 6
- resident: bfloat16 [38912, 8192], P(('out', 'inp')), may hold values from -6 to 6
Outputs:
- refreshed: bfloat16 [38912, 8192], P(('out', 'inp'))
All inputs are finite; a program needn't handle non-finite values.
Results may differ from a plain program's by a relative error of at most 0.001.
Values may be sent and summed in bfloat16 or wider, within the bound.
A program may use at most 64 MiB of HBM per device.

v0:
```python
import jax
import jax.numpy as jnp
from jax import lax
from jax.sharding import PartitionSpec as P


def swapped(value, axis, distance):
    mask = 2**distance
    pairs = [(source, source ^ mask) for source in range(lax.axis_size(axis))]
    return lax.ppermute(value, axis, pairs)


def sylvester(order):
    indices = lax.iota(jnp.int32, order)
    intersection = indices[:, None] & indices[None, :]
    parity = jnp.zeros((order, order), jnp.int32)
    for shift in range(order.bit_length()):
        parity = parity ^ intersection >> shift & 1
    return (1 - 2 * parity).astype(jnp.float32)


def shards(weight_delta, resident):
    local_rows = weight_delta.shape[0]
    groups = lax.axis_size("inp")
    total_rows = local_rows * groups
    factor = 1.0 / jnp.sqrt(jnp.float32(total_rows))
    local_matrix = sylvester(local_rows).astype(jnp.bfloat16)
    rotated_local = jnp.dot(local_matrix, weight_delta, preferred_element_type=jnp.float32)
    position = lax.axis_index("inp")
    for level in range(groups.bit_length() - 1):
        partner = swapped(rotated_local, "inp", level)
        upper_half = position >> level & 1 == 1
        rotated_local = jnp.where(upper_half, partner - rotated_local, rotated_local + partner)
    rotated_all = lax.all_to_all(rotated_local, "inp", split_axis=1, concat_axis=0, tiled=True)
    rotated_all = rotated_all * factor
    return (resident.astype(jnp.float32) + rotated_all.T).astype(jnp.bfloat16)


def solution(mesh):
    placed = (P("inp", "out"), P(("out", "inp"), None))
    return jax.shard_map(
        shards, mesh=mesh, in_specs=placed, out_specs=P(("out", "inp"), None), check_vma=False
    )
```

profile of v0, /device:TPU:1, one launch (start us, length us, event | category | flops | bytes accessed | tf_op | source)
XLA Modules:
  0.0 561.6 jit_solution(6825219176224571623)
XLA Ops:
  0.0 0.0 copy-start
  0.0 1.7 copy-done
  1.7 3.3 fusion.1
  5.0 3.2 collective-permute-start
  8.2 8.3 %collective-permute-done = f32[256,4864]{1,0:T(8,128)} collective-permute-done((f32[256,4864]{1,0:T(8,128)}, f32[256,4864]{1,0:T(8,128)}, u32[]{:S(2)}, u32[]{:S(2)}) %collective-permute-start) | collective-permute-done | bytes 4980768 | tf_op jit(solution)/shard_map/ppermute | solution.py:10
  16.5 6.7 %add_select_fusion.4 = f32[256,4864]{1,0:T(8,128)} fusion(f32[256,4864]{1,0:T(8,128)} %fusion.1, f32[256,4864]{1,0:T(8,128)} %collective-permute-done, pred[]{:T(512)S(6)} %eq.19), kind=kLoop, calls=%fused_computation.7 | loop fusion | flops 3735552 | bytes 14942209 | tf_op jit(solution)/shard_map/jit(_where)/select_n | solution.py:33
  23.2 0.0 collective-permute-start.1
  23.2 109.0 %collective-permute-done.1 = f32[256,4864]{1,0:T(8,128)} collective-permute-done((f32[256,4864]{1,0:T(8,128)}, f32[256,4864]{1,0:T(8,128)}, u32[]{:S(2)}, u32[]{:S(2)}) %collective-permute-start.1) | collective-permute-done | bytes 4980768 | tf_op jit(solution)/shard_map/ppermute | solution.py:10
  132.1 6.7 %add_select_fusion.3 = f32[256,4864]{1,0:T(8,128)} fusion(f32[256,4864]{1,0:T(8,128)} %add_select_fusion.4, f32[256,4864]{1,0:T(8,128)} %collective-permute-done.1, pred[]{:T(512)S(6)} %eq.18), kind=kLoop, calls=%fused_computation.6 | loop fusion | flops 3735552 | bytes 14942209 | tf_op jit(solution)/shard_map/jit(_where)/select_n | solution.py:33
  138.8 1.0 collective-permute-start.2
  139.8 108.5 %collective-permute-done.2 = f32[256,4864]{1,0:T(8,128)} collective-permute-done((f32[256,4864]{1,0:T(8,128)}, f32[256,4864]{1,0:T(8,128)}, u32[]{:S(2)}, u32[]{:S(2)}) %collective-permute-start.2) | collective-permute-done | bytes 4980768 | tf_op jit(solution)/shard_map/ppermute | solution.py:10
  248.4 6.7 %add_select_fusion.2 = f32[256,4864]{1,0:T(8,128)} fusion(f32[256,4864]{1,0:T(8,128)} %add_select_fusion.3, f32[256,4864]{1,0:T(8,128)} %collective-permute-done.2, pred[]{:T(512)S(6)} %eq.17), kind=kLoop, calls=%fused_computation.5 | loop fusion | flops 3735552 | bytes 14942209 | tf_op jit(solution)/shard_map/jit(_where)/select_n | solution.py:33
  255.1 0.0 collective-permute-start.3
  255.1 107.1 %collective-permute-done.3 = f32[256,4864]{1,0:T(8,128)} collective-permute-done((f32[256,4864]{1,0:T(8,128)}, f32[256,4864]{1,0:T(8,128)}, u32[]{:S(2)}, u32[]{:S(2)}) %collective-permute-start.3) | collective-permute-done | bytes 4980768 | tf_op jit(solution)/shard_map/ppermute | solution.py:10
  362.2 6.7 %add_select_fusion.1 = f32[256,4864]{1,0:T(8,128)} fusion(f32[256,4864]{1,0:T(8,128)} %add_select_fusion.2, f32[256,4864]{1,0:T(8,128)} %collective-permute-done.3, pred[]{:T(512)S(6)} %eq.16), kind=kLoop, calls=%fused_computation.4 | loop fusion | flops 3735552 | bytes 14942209 | tf_op jit(solution)/shard_map/jit(_where)/select_n | solution.py:33
  368.9 1.2 collective-permute-start.4
  370.0 106.5 %collective-permute-done.4 = f32[256,4864]{1,0:T(8,128)} collective-permute-done((f32[256,4864]{1,0:T(8,128)}, f32[256,4864]{1,0:T(8,128)}, u32[]{:S(2)}, u32[]{:S(2)}) %collective-permute-start.4) | collective-permute-done | bytes 4980768 | tf_op jit(solution)/shard_map/ppermute | solution.py:10
  476.6 6.7 %add_select_fusion = f32[256,4864]{1,0:T(8,128)} fusion(f32[256,4864]{1,0:T(8,128)} %add_select_fusion.1, f32[256,4864]{1,0:T(8,128)} %collective-permute-done.4, pred[]{:T(512)S(6)} %eq.15), kind=kLoop, calls=%fused_computation.3 | loop fusion | flops 3735552 | bytes 14942209 | tf_op jit(solution)/shard_map/jit(_where)/select_n | solution.py:33
  483.3 5.8 %copy.5 = f32[256,4864]{0,1:T(8,128)} copy(f32[256,4864]{1,0:T(8,128)} %add_select_fusion) | data formatting | bytes 9961472 | tf_op jit(solution)/shard_map/jit(_where)/select_n | solution.py:33
  489.0 68.5 %all_to_all.13 = f32[256,32,152]{0,2,1:T(8,128)S(1)} all-to-all(f32[256,32,152]{0,2,1:T(8,128)} %bitcast.10), channel_id=1, replica_groups=mesh['out'=8,'inp'=32] {'inp'}, dimensions={1} | all-to-all | bytes 9961472 | tf_op jit(solution)/shard_map/all_to_all | solution.py:34
  557.5 0.4 multiply_bitcast_fusion
  558.0 0.0 copy-start.2
  558.0 0.6 copy.7
  558.5 0.0 copy-start.1
  558.5 1.1 copy-done.2
  559.7 1.9 fusion
  561.6 0.0 copy-done.1
Async XLA Ops:
  0.0 1.7 copy-start
  5.0 11.5 %collective-permute-start = (f32[256,4864]{1,0:T(8,128)}, f32[256,4864]{1,0:T(8,128)}, u32[]{:S(2)}, u32[]{:S(2)}) collective-permute-start(f32[256,4864]{1,0:T(8,128)} %fusion.1), channel_id=1, source_target_pairs={{0,1},{1,0},{2,3},{3,2},{4,5},{5,4},{6,7},{7,6},{8,9},{9,8},{10,11... | collective-permute-start | bytes 14942216 | tf_op jit(solution)/shard_map/ppermute | solution.py:10
  23.2 109.0 %collective-permute-start.1 = (f32[256,4864]{1,0:T(8,128)}, f32[256,4864]{1,0:T(8,128)}, u32[]{:S(2)}, u32[]{:S(2)}) collective-permute-start(f32[256,4864]{1,0:T(8,128)} %add_select_fusion.4), channel_id=1, source_target_pairs={{0,2},{1,3},{2,0},{3,1},{4,6},{5,7},{6,4},{7,5},{8,10},{9,11},{10,... | collective-permute-start | bytes 14942216 | tf_op jit(solution)/shard_map/ppermute | solution.py:10
  138.8 109.5 %collective-permute-start.2 = (f32[256,4864]{1,0:T(8,128)}, f32[256,4864]{1,0:T(8,128)}, u32[]{:S(2)}, u32[]{:S(2)}) collective-permute-start(f32[256,4864]{1,0:T(8,128)} %add_select_fusion.3), channel_id=1, source_target_pairs={{0,4},{1,5},{2,6},{3,7},{4,0},{5,1},{6,2},{7,3},{8,12},{9,13},{10,... | collective-permute-start | bytes 14942216 | tf_op jit(solution)/shard_map/ppermute | solution.py:10
  255.1 107.1 %collective-permute-start.3 = (f32[256,4864]{1,0:T(8,128)}, f32[256,4864]{1,0:T(8,128)}, u32[]{:S(2)}, u32[]{:S(2)}) collective-permute-start(f32[256,4864]{1,0:T(8,128)} %add_select_fusion.2), channel_id=1, source_target_pairs={{0,8},{1,9},{2,10},{3,11},{4,12},{5,13},{6,14},{7,15},{8,0},{9,1},... | collective-permute-start | bytes 14942216 | tf_op jit(solution)/shard_map/ppermute | solution.py:10
  368.9 107.7 %collective-permute-start.4 = (f32[256,4864]{1,0:T(8,128)}, f32[256,4864]{1,0:T(8,128)}, u32[]{:S(2)}, u32[]{:S(2)}) collective-permute-start(f32[256,4864]{1,0:T(8,128)} %add_select_fusion.1), channel_id=1, source_target_pairs={{0,16},{1,17},{2,18},{3,19},{4,20},{5,21},{6,22},{7,23},{8,24},{9,... | collective-permute-start | bytes 14942216 | tf_op jit(solution)/shard_map/ppermute | solution.py:10
  558.0 1.7 copy-start.2
  558.5 3.1 copy-start.1
where the time goes:
time: 562 us
  waiting for transfers between devices  439 us (78%)
  blocking collectives  68.5 us (12%)
  other arithmetic  35.8 us (6%)
  local copies, waits for them, and re-layouts  9.16 us (2%)
    ppermute x5, waiting for transfers between devices, swapped(): return lax.ppermute(value, axis, pairs)  439 us
    all_to_all x1, blocking collectives, shards(): lax.all_to_all(rotated_local, 'inp', split_axis=1, concat_axis=0, tiled=T...  68.5 us
    select_n x5, other arithmetic, shards(): jnp.where(upper_half, partner - rotated_local, rotated_local + partner)  33.5 us
  transfers between devices with their start and end apart: 5, of which 5 were waited for; matrix products, arithmetic and copies ran while one was open for 0% of the time, Pallas kernels for 0%

commit v1 on v0

v1 whole, which is shorter than its diff:
```python
import functools

import jax
import jax.numpy as jnp
from jax import lax
from jax.experimental import pallas as pl
from jax.experimental.pallas import tpu as pltpu
from jax.sharding import PartitionSpec as P

LANES = 128
SIDE = 4
CORES = 2
CHUNK = 16
FAR_A = ((2, 0), (3, 1))
FAR_B = ((0, 1), (3, 2))
MESH = pl.DeviceIdType.MESH
def sylvester(order):
    rows = lax.broadcasted_iota(jnp.int32, (order, order), 0)
    cols = lax.broadcasted_iota(jnp.int32, (order, order), 1)
    parity = rows & cols
    for shift in (4, 2, 1):
        parity = parity ^ (parity >> shift)
    return (1 - 2 * (parity & 1)).astype(jnp.float32).astype(jnp.bfloat16)


def selection(order, window, shift):
    rows = lax.broadcasted_iota(jnp.int32, (order, window), 0)
    cols = lax.broadcasted_iota(jnp.int32, (order, window), 1)
    return jnp.where(cols == rows + shift, 1.0, 0.0).astype(jnp.bfloat16)


def butterfly(values):
    values = list(values)
    stride = 1
    while stride < len(values):
        for at in range(len(values)):
            if at & stride == 0:
                first, second = values[at], values[at + stride]
                values[at], values[at + stride] = first + second, first - second
        stride *= 2
    return values


def exchange_kernel(
    update_hbm, work_ref, update, sending, middle, relay, received,
    load_sem, send_sems, middle_sems, relay_sems, recv_sems,
):
    cols = update.shape[1]
    stacked = received.shape[1]
    feats = stacked // 2
    groups = cols // feats
    window = -(-(CORES * feats + LANES - 1) // LANES) * LANES
    me = lax.axis_index("inp")
    core = me % CORES
    my_chip = me // CORES
    my_x = my_chip % SIDE
    my_y = my_chip // SIDE
    my_a = my_x + core * (my_y - my_x)
    my_b = my_y + core * (my_x - my_y)

    def chip_at(da, db):
        a, b = (my_a + da) % SIDE, (my_b + db) % SIDE
        x, y = a + core * (b - a), b + core * (a - b)
        return y * SIDE + x

    def device_at(da, db, c):
        return chip_at(da, db) * CORES + c

    load = pltpu.make_async_copy(update_hbm, update, load_sem)
    load.start()
    barrier = pltpu.get_barrier_semaphore()
    others = [device_at(da, db, c) for da, db in ((1, 0), (3, 0), (0, 1), (0, 3)) for c in range(CORES)]
    others.append(device_at(0, 0, 1 - core))
    for device in others:
        pl.semaphore_signal(barrier, inc=1, device_id={"inp": device}, device_id_type=MESH)

    def make(da, db):
        chip = chip_at(da, db)
        first = jnp.minimum(chip * CORES * feats // LANES, (cols - window) // LANES)
        shift = chip * CORES * feats - first * LANES
        columns = update[:, pl.ds(pl.multiple_of(first * LANES, LANES), window)]
        turned = lax.dot_general(
            selection(CORES * feats, window, shift), columns, (((1,), (1,)), ((), ())),
            preferred_element_type=jnp.float32,
        )
        for c in range(CORES):
            rows = turned[c * feats : (c + 1) * feats]
            sending[da, db, c] = jnp.concatenate([rows[:, :LANES], rows[:, LANES:]], axis=0).astype(sending.dtype)

    sends = []

    def send(src, dst, sem, device):
        copy = pltpu.make_async_remote_copy(
            src_ref=src, dst_ref=dst, send_sem=send_sems.at[len(sends)], recv_sem=sem,
            device_id={"inp": device}, device_id_type=MESH,
        )
        copy.start()
        sends.append(copy)

    def wait(dst, sem):
        pltpu.make_async_remote_copy(
            src_ref=dst, dst_ref=dst, send_sem=send_sems.at[0], recv_sem=sem,
            device_id={"inp": me}, device_id_type=MESH,
        ).wait_recv()

    def held(da, db):
        return sending.at[da, db] if da == 0 else middle.at[da, db]

    def to_middle(src, step, da, db):
        send(src, middle.at[da, db], middle_sems.at[da, db], device_at(step, 0, core))

    def to_relay(src, step, way, slot):
        da, db = (step, 0) if way < 2 else (0, step)
        send(src, relay.at[way, slot], relay_sems.at[way, slot], device_at(da, db, core))

    def to_end(src, step, da, db):
        source = device_at(SIDE - da, db, core)
        for c in range(CORES):
            send(src.at[c], received.at[source], recv_sems.at[source], device_at(0, step, c))

    def wait_middle(da, db):
        wait(middle.at[da, db], middle_sems.at[da, db])

    def hand_on(way, slot):
        wait(relay.at[way, slot], relay_sems.at[way, slot])
        step = (1, 3)[way % 2]
        if way < 2:
            to_middle(relay.at[way, slot], step, 2, FAR_A[way][slot])
        else:
            to_end(relay.at[way, slot], step, FAR_B[way - 2][slot], SIDE - step)

    def home(da):
        block = held(da, 0)
        source = device_at(SIDE - da, 0, core)
        send(block.at[1 - core], received.at[source], recv_sems.at[source], device_at(0, 0, 1 - core))
        received[source] = block[core]

    load.wait()
    for way in range(2):
        make(2, FAR_A[way][0])
    pl.semaphore_wait(barrier, len(others))

    for slot in range(2):
        for way in range(2):
            db = FAR_A[way][slot]
            if slot > 0:
                make(2, db)
            to_relay(sending.at[2, db], (1, 3)[way], way, slot)

    def along(db):
        for da in (1, 3):
            make(da, db)
            to_middle(sending.at[da, db], da, da, db)

    along(2)
    along(1)
    hand_on(0, 0)
    hand_on(1, 0)
    along(3)
    hand_on(0, 1)
    hand_on(1, 1)
    along(0)

    make(0, 2)
    to_relay(held(0, 2), 1, 2, 0)
    wait_middle(3, 2)
    to_relay(held(3, 2), 3, 3, 0)
    wait_middle(1, 2)
    to_relay(held(1, 2), 1, 2, 1)
    for db in (1, 3):
        make(0, db)
        to_end(held(0, db), db, 0, 0)
    wait_middle(2, 2)
    to_relay(held(2, 2), 3, 3, 1)
    for da in (1, 3):
        for db in (1, 3):
            wait_middle(da, db)
            to_end(held(da, db), db, da, 0)
    make(0, 0)
    home(0)
    hand_on(2, 0)
    hand_on(3, 0)
    for db in (1, 3):
        wait_middle(2, db)
        to_end(held(2, db), db, 2, 0)
    for da in (1, 3, 2):
        wait_middle(da, 0)
        home(da)
    hand_on(2, 1)
    hand_on(3, 1)

    matrix = sylvester(LANES)
    for da, db in ((0, 0), (1, 0), (3, 0), (2, 0), (0, 1), (0, 3), (1, 1), (3, 3), (1, 3), (3, 1),
                   (0, 2), (2, 1), (2, 3), (1, 2), (3, 2), (2, 2)):
        from_x, from_y = (my_x + da) % SIDE, (my_y + db) % SIDE
        chip = from_y * SIDE + from_x
        for c in range(CORES):
            if (db, da)[c] == 0:

                @pl.when(core != c)
                def _(source=chip * CORES + c):
                    wait(received.at[source], recv_sems.at[source])
            else:
                wait(received.at[chip * CORES + c], recv_sems.at[chip * CORES + c])
        parts = []
        for c in range(CORES):
            both = jnp.dot(received[chip * CORES + c], matrix, preferred_element_type=jnp.float32)
            parts += [both[:feats], both[feats:]]
        for at, value in enumerate(butterfly(parts)):
            work_ref[from_y, from_x, at] = value

    for copy in sends:
        copy.wait_send()


def finish_kernel(work_ref, resident, out_hbm, out, out_sems):
    feats, width = out.shape
    factor = 1.0 / jnp.sqrt(jnp.float32(width))
    whole = feats // CHUNK

    def store(chunk, rows):
        return pltpu.make_async_copy(out.at[rows], out_hbm.at[rows], out_sems.at[chunk])

    def finish(rows):
        for at in range(2 * CORES):
            values = butterfly([work_ref[y, x, at, rows, :] for y in range(SIDE) for x in range(SIDE)])
            for chip, value in enumerate(values):
                cols = pl.ds((chip * 2 * CORES + at) * LANES, LANES)
                total = resident[rows, cols].astype(jnp.float32) + value * factor
                out[rows, cols] = total.astype(out.dtype)

    @pl.loop(0, whole)
    def _(chunk):
        rows = pl.ds(pl.multiple_of(chunk * CHUNK, CHUNK), CHUNK)
        finish(rows)
        store(chunk, rows).start()

    rest = pl.ds(whole * CHUNK, feats % CHUNK)
    if feats % CHUNK:
        finish(rest)
        store(whole, rest).start()
        store(whole, rest).wait()

    @pl.loop(0, whole)
    def _(chunk):
        store(chunk, pl.ds(pl.multiple_of(chunk * CHUNK, CHUNK), CHUNK)).wait()


def shards(weight_delta, resident):
    rows, cols = weight_delta.shape
    groups = lax.axis_size("inp")
    feats = cols // groups
    size = rows * cols
    work = pl.pallas_call(
        exchange_kernel,
        out_shape=pltpu.VMEM((SIDE, SIDE, 2 * CORES, feats, LANES), jnp.float32),
        in_specs=[pl.BlockSpec(memory_space=pl.ANY)],
        out_specs=pl.BlockSpec(memory_space=pltpu.VMEM),
        scratch_shapes=[
            pltpu.VMEM((rows, cols), weight_delta.dtype),
            pltpu.VMEM((SIDE, SIDE, CORES, 2 * feats, LANES), weight_delta.dtype),
            pltpu.VMEM((SIDE, SIDE, CORES, 2 * feats, LANES), weight_delta.dtype),
            pltpu.VMEM((4, 2, CORES, 2 * feats, LANES), weight_delta.dtype),
            pltpu.VMEM((groups, 2 * feats, LANES), weight_delta.dtype),
            pltpu.SemaphoreType.DMA,
            pltpu.SemaphoreType.DMA((64,)),
            pltpu.SemaphoreType.DMA((SIDE, SIDE)),
            pltpu.SemaphoreType.DMA((4, 2)),
            pltpu.SemaphoreType.DMA((groups,)),
        ],
        compiler_params=pltpu.CompilerParams(
            collective_id=0, has_side_effects=True, vmem_limit_bytes=32 * 1024 * 1024
        ),
        cost_estimate=pl.CostEstimate(flops=2 * size * (rows + LANES), bytes_accessed=2 * size, transcendentals=0),
    )(pltpu.with_memory_space_constraint(weight_delta, pltpu.HBM))
    return pl.pallas_call(
        finish_kernel,
        out_shape=jax.ShapeDtypeStruct(resident.shape, resident.dtype),
        in_specs=[pl.BlockSpec(memory_space=pltpu.VMEM)] * 2,
        out_specs=pl.BlockSpec(memory_space=pl.ANY),
        scratch_shapes=[
            pltpu.VMEM(resident.shape, resident.dtype),
            pltpu.SemaphoreType.DMA((-(-feats // CHUNK),)),
        ],
        compiler_params=pltpu.CompilerParams(vmem_limit_bytes=32 * 1024 * 1024),
        cost_estimate=pl.CostEstimate(flops=6 * size, bytes_accessed=4 * size, transcendentals=0),
    )(work, resident)


def solution(mesh):
    placed = (P("inp", "out"), P(("out", "inp"), None))
    return jax.shard_map(
        shards, mesh=mesh, in_specs=placed, out_specs=P(("out", "inp"), None), check_vma=False
    )
```

time: 562 us -> 39.1 us (0.07)
  waiting for transfers between devices: 439 us -> 0 us
  blocking collectives: 68.5 us -> 0 us
  Pallas kernels: 0 us -> 39 us
  other arithmetic: 35.8 us -> 0 us
  local copies, waits for them, and re-layouts: 9.16 us -> 0.01 us
    ppermute x5 -> x0, waiting for transfers between devices: 439 us -> none  [swapped(): return lax.ppermute(value, axis, pairs)]
    all_to_all x1 -> x0, blocking collectives: 68.5 us -> none  [shards(): lax.all_to_all(rotated_local, 'inp', split_axis=1, concat_axis=0, tiled=T...]
    pallas_call x0 -> x2, Pallas kernels: none -> 39 us  [the longest x1 36.9 us: shards(): pl.pallas_call(exchange_kernel, out_shape=pltpu.VMEM((SIDE, SIDE, 2 * COR...]
    select_n x5 -> x0, other arithmetic: 33.5 us -> none  [shards(): jnp.where(upper_half, partner - rotated_local, rotated_local + partner)]
    select_n x1 -> x0, local copies, waits for them, and re-layouts: 5.78 us -> none  [shards(): jnp.where(upper_half, partner - rotated_local, rotated_local + partner)]
  transfers between devices with their start and end apart: 5 -> 0, of which waited for: 5 -> 0; matrix products, arithmetic and copies ran while one was open for 0% -> 0% of each run, Pallas kernels for 0% -> 0%
where the time goes in v1:
time: 39.1 us; the launch traced here: 39 us
  Pallas kernels  39 us (100%)
    pallas_call x1, Pallas kernels, shards(): pl.pallas_call(exchange_kernel, out_shape=pltpu.VMEM((SIDE, SIDE, 2 * COR...  36.9 us
    pallas_call x1, Pallas kernels, shards(): pl.pallas_call(finish_kernel, out_shape=jax.ShapeDtypeStruct(resident.sha...  2.14 us

profile of v1, /device:TPU:1, one launch (start us, length us, event | category | flops | bytes accessed | tf_op | source)
XLA Modules:
  0.0 39.0 jit_solution(14221020947718190040)
XLA Ops:
  0.0 0.0 copy-start
  0.0 36.9 %shard_map.28.work_ref = f32[4,4,4,152,128]{4,3,2,1,0:T(8,128)S(1)} custom-call(bf16[256,4864]{1,0:T(8,128)(2,1)} %update_hbm.1), custom_call_target="tpu_custom_call" | custom-call | flops 956301312 | bytes 2490368 | tf_op jit(solution)/shard_map/pallas_call | solution.py:254
  36.9 0.0 copy-done
  36.9 2.1 %shard_map.29 = bf16[152,8192]{1,0:T(8,128)(2,1)} custom-call(f32[4,4,4,152,128]{4,3,2,1,0:T(8,128)S(1)} %shard_map.28.work_ref, bf16[152,8192]{1,0:T(8,128)(2,1)S(1)} %copy-done), custom_call_target="tpu_custom_call" | custom-call | flops 7471104 | bytes 4980736 | tf_op jit(solution)/shard_map/pallas_call | solution.py:276
Async XLA Ops:
  0.0 36.9 %copy-start = (bf16[152,8192]{1,0:T(8,128)(2,1)S(1)}, bf16[152,8192]{1,0:T(8,128)(2,1)}, u32[]{:S(2)}) copy-start(bf16[152,8192]{1,0:T(8,128)(2,1)} %resident.1) | copy-start | bytes 7471108

commit v2 on v1

--- a/solution.py
+++ b/solution.py
@@ -13,7 +13,15 @@
 CHUNK = 16
 FAR_A = ((2, 0), (3, 1))
 FAR_B = ((0, 1), (3, 2))
+ARRIVALS = (
+    (0, 0), (1, 0), (3, 0), (2, 0), (0, 2), (1, 1), (3, 1), (3, 2),
+    (1, 2), (1, 3), (3, 3), (2, 2), (2, 3), (2, 1), (0, 1), (0, 3),
+)
 MESH = pl.DeviceIdType.MESH
+def window_of(feats):
+    return -(-(CORES * feats + LANES - 1) // LANES) * LANES
+
+
 def sylvester(order):
     rows = lax.broadcasted_iota(jnp.int32, (order, order), 0)
     cols = lax.broadcasted_iota(jnp.int32, (order, order), 1)
@@ -42,14 +50,14 @@
 
 
 def exchange_kernel(
-    update_hbm, work_ref, update, sending, middle, relay, received,
-    load_sem, send_sems, middle_sems, relay_sems, recv_sems,
+    update_hbm, work_ref, update, early, sending, middle, relay, received,
+    load_sem, early_sems, send_sems, middle_sems, relay_sems, recv_sems,
 ):
     cols = update.shape[1]
     stacked = received.shape[1]
     feats = stacked // 2
     groups = cols // feats
-    window = -(-(CORES * feats + LANES - 1) // LANES) * LANES
+    window = window_of(feats)
     me = lax.axis_index("inp")
     core = me % CORES
     my_chip = me // CORES
@@ -66,21 +74,30 @@
     def device_at(da, db, c):
         return chip_at(da, db) * CORES + c
 
+    def window_at(da, db):
+        chip = chip_at(da, db)
+        first = jnp.minimum(chip * CORES * feats // LANES, (cols - window) // LANES)
+        return pl.ds(pl.multiple_of(first * LANES, LANES), window), chip * CORES * feats - first * LANES
+
+    firsts = [
+        pltpu.make_async_copy(update_hbm.at[:, window_at(2, FAR_A[way][0])[0]], early.at[way], early_sems.at[way])
+        for way in range(2)
+    ]
     load = pltpu.make_async_copy(update_hbm, update, load_sem)
-    load.start()
+    for copy in (*firsts, load):
+        copy.start()
     barrier = pltpu.get_barrier_semaphore()
     others = [device_at(da, db, c) for da, db in ((1, 0), (3, 0), (0, 1), (0, 3)) for c in range(CORES)]
     others.append(device_at(0, 0, 1 - core))
     for device in others:
         pl.semaphore_signal(barrier, inc=1, device_id={"inp": device}, device_id_type=MESH)
 
-    def make(da, db):
-        chip = chip_at(da, db)
-        first = jnp.minimum(chip * CORES * feats // LANES, (cols - window) // LANES)
-        shift = chip * CORES * feats - first * LANES
-        columns = update[:, pl.ds(pl.multiple_of(first * LANES, LANES), window)]
+    def make(da, db, columns=None):
+        at, shift = window_at(da, db)
         turned = lax.dot_general(
-            selection(CORES * feats, window, shift), columns, (((1,), (1,)), ((), ())),
+            selection(CORES * feats, window, shift),
+            update[:, at] if columns is None else columns,
+            (((1,), (1,)), ((), ())),
             preferred_element_type=jnp.float32,
         )
         for c in range(CORES):
@@ -106,10 +123,15 @@
     def held(da, db):
         return sending.at[da, db] if da == 0 else middle.at[da, db]
 
+    def wait_held(da, db):
+        if da != 0:
+            wait(middle.at[da, db], middle_sems.at[da, db])
+
     def to_middle(src, step, da, db):
         send(src, middle.at[da, db], middle_sems.at[da, db], device_at(step, 0, core))
 
-    def to_relay(src, step, way, slot):
+    def to_relay(src, way, slot):
+        step = (1, 3)[way % 2]
         da, db = (step, 0) if way < 2 else (0, step)
         send(src, relay.at[way, slot], relay_sems.at[way, slot], device_at(da, db, core))
 
@@ -118,8 +140,24 @@
         for c in range(CORES):
             send(src.at[c], received.at[source], recv_sems.at[source], device_at(0, step, c))
 
-    def wait_middle(da, db):
-        wait(middle.at[da, db], middle_sems.at[da, db])
+    def far_a(slot):
+        for way in range(2):
+            to_relay(sending.at[2, FAR_A[way][slot]], way, slot)
+
+    def near_a(db):
+        for da in (1, 3):
+            make(da, db)
+        for da in (1, 3):
+            to_middle(sending.at[da, db], da, da, db)
+
+    def far_b(way, slot):
+        da = FAR_B[way - 2][slot]
+        wait_held(da, 2)
+        to_relay(held(da, 2), way, slot)
+
+    def near_b(da, db):
+        wait_held(da, db)
+        to_end(held(da, db), db, da, 0)
 
     def hand_on(way, slot):
         wait(relay.at[way, slot], relay_sems.at[way, slot])
@@ -130,84 +168,79 @@
             to_end(relay.at[way, slot], step, FAR_B[way - 2][slot], SIDE - step)
 
     def home(da):
+        wait_held(da, 0)
         block = held(da, 0)
         source = device_at(SIDE - da, 0, core)
         send(block.at[1 - core], received.at[source], recv_sems.at[source], device_at(0, 0, 1 - core))
         received[source] = block[core]
 
+    for way in range(2):
+        firsts[way].wait()
+        make(2, FAR_A[way][0], early[way])
+    pl.semaphore_wait(barrier, len(others))
+
+    far_a(0)
     load.wait()
+    make(0, 2)
+    far_b(2, 0)
+    near_a(2)
     for way in range(2):
-        make(2, FAR_A[way][0])
-    pl.semaphore_wait(barrier, len(others))
-
-    for slot in range(2):
-        for way in range(2):
-            db = FAR_A[way][slot]
-            if slot > 0:
-                make(2, db)
-            to_relay(sending.at[2, db], (1, 3)[way], way, slot)
-
-    def along(db):
-        for da in (1, 3):
-            make(da, db)
-            to_middle(sending.at[da, db], da, da, db)
-
-    along(2)
-    along(1)
+        make(2, FAR_A[way][1])
+    far_a(1)
     hand_on(0, 0)
     hand_on(1, 0)
-    along(3)
+    near_a(1)
+    far_b(3, 0)
+    far_b(2, 1)
+    near_a(3)
     hand_on(0, 1)
     hand_on(1, 1)
-    along(0)
-
-    make(0, 2)
-    to_relay(held(0, 2), 1, 2, 0)
-    wait_middle(3, 2)
-    to_relay(held(3, 2), 3, 3, 0)
-    wait_middle(1, 2)
-    to_relay(held(1, 2), 1, 2, 1)
-    for db in (1, 3):
-        make(0, db)
-        to_end(held(0, db), db, 0, 0)
-    wait_middle(2, 2)
-    to_relay(held(2, 2), 3, 3, 1)
-    for da in (1, 3):
-        for db in (1, 3):
-            wait_middle(da, db)
-            to_end(held(da, db), db, da, 0)
+    far_b(3, 1)
+    hand_on(2, 0)
+    near_a(0)
+    near_b(1, 1)
+    near_b(3, 1)
+    hand_on(3, 0)
+    hand_on(2, 1)
+    near_b(1, 3)
+    near_b(3, 3)
+    hand_on(3, 1)
+    near_b(2, 3)
+    near_b(2, 1)
+    make(0, 1)
+    make(0, 3)
+    near_b(0, 1)
+    near_b(0, 3)
     make(0, 0)
-    home(0)
-    hand_on(2, 0)
-    hand_on(3, 0)
-    for db in (1, 3):
-        wait_middle(2, db)
-        to_end(held(2, db), db, 2, 0)
-    for da in (1, 3, 2):
-        wait_middle(da, 0)
+    for da in (0, 1, 3, 2):
         home(da)
-    hand_on(2, 1)
-    hand_on(3, 1)
 
     matrix = sylvester(LANES)
-    for da, db in ((0, 0), (1, 0), (3, 0), (2, 0), (0, 1), (0, 3), (1, 1), (3, 3), (1, 3), (3, 1),
-                   (0, 2), (2, 1), (2, 3), (1, 2), (3, 2), (2, 2)):
-        from_x, from_y = (my_x + da) % SIDE, (my_y + db) % SIDE
-        chip = from_y * SIDE + from_x
+
+    def rotate(da, db, c):
+        x, y = (da, db)[c], (db, da)[c]
+        from_x, from_y = (my_x + SIDE - x) % SIDE, (my_y + SIDE - y) % SIDE
+        source = (from_y * SIDE + from_x) * CORES + c
+        if db == 0:
+            @pl.when(core != c)
+            def _():
+                wait(received.at[source], recv_sems.at[source])
+        else:
+            wait(received.at[source], recv_sems.at[source])
+        both = jnp.dot(received[source], matrix, preferred_element_type=jnp.float32)
+        halves = both[:feats] + both[feats:], both[:feats] - both[feats:]
+        if ARRIVALS.index((da, db)) < ARRIVALS.index((db, da)) or (da == db and c == 0):
+            for half in range(2):
+                work_ref[from_y, from_x, 2 * c + half] = halves[half]
+        else:
+            for half in range(2):
+                there = work_ref[from_y, from_x, 2 * (1 - c) + half]
+                work_ref[from_y, from_x, half] = halves[half] + there
+                work_ref[from_y, from_x, 2 + half] = halves[half] - there if c == 0 else there - halves[half]
+
+    for da, db in ARRIVALS:
         for c in range(CORES):
-            if (db, da)[c] == 0:
-
-                @pl.when(core != c)
-                def _(source=chip * CORES + c):
-                    wait(received.at[source], recv_sems.at[source])
-            else:
-                wait(received.at[chip * CORES + c], recv_sems.at[chip * CORES + c])
-        parts = []
-        for c in range(CORES):
-            both = jnp.dot(received[chip * CORES + c], matrix, preferred_element_type=jnp.float32)
-            parts += [both[:feats], both[feats:]]
-        for at, value in enumerate(butterfly(parts)):
-            work_ref[from_y, from_x, at] = value
+            rotate(da, db, c)
 
     for copy in sends:
         copy.wait_send()
@@ -258,11 +291,13 @@
         out_specs=pl.BlockSpec(memory_space=pltpu.VMEM),
         scratch_shapes=[
             pltpu.VMEM((rows, cols), weight_delta.dtype),
+            pltpu.VMEM((2, rows, window_of(feats)), weight_delta.dtype),
             pltpu.VMEM((SIDE, SIDE, CORES, 2 * feats, LANES), weight_delta.dtype),
             pltpu.VMEM((SIDE, SIDE, CORES, 2 * feats, LANES), weight_delta.dtype),
             pltpu.VMEM((4, 2, CORES, 2 * feats, LANES), weight_delta.dtype),
             pltpu.VMEM((groups, 2 * feats, LANES), weight_delta.dtype),
             pltpu.SemaphoreType.DMA,
+            pltpu.SemaphoreType.DMA((2,)),
             pltpu.SemaphoreType.DMA((64,)),
             pltpu.SemaphoreType.DMA((SIDE, SIDE)),
             pltpu.SemaphoreType.DMA((4, 2)),

time: 39.1 us -> 41 us (1.049)
  Pallas kernels: 39 us -> 40.9 us
    pallas_call x1, Pallas kernels: 36.9 us -> 38.8 us  [shards(): pl.pallas_call(exchange_kernel, out_shape=pltpu.VMEM((SIDE, SIDE, 2 * COR...]
where the time goes in v2:
time: 41 us; the launch traced here: 40.9 us
  Pallas kernels  40.9 us (100%)
    pallas_call x1, Pallas kernels, shards(): pl.pallas_call(exchange_kernel, out_shape=pltpu.VMEM((SIDE, SIDE, 2 * COR...  38.8 us
    pallas_call x1, Pallas kernels, shards(): pl.pallas_call(finish_kernel, out_shape=jax.ShapeDtypeStruct(resident.sha...  2.14 us

profile of v2, /device:TPU:1, one launch (start us, length us, event | category | flops | bytes accessed | tf_op | source)
XLA Modules:
  0.0 40.9 jit_solution(11956492567808958780)
XLA Ops:
  0.0 0.0 copy-start
  0.0 38.8 %shard_map.28.work_ref = f32[4,4,4,152,128]{4,3,2,1,0:T(8,128)S(1)} custom-call(bf16[256,4864]{1,0:T(8,128)(2,1)} %update_hbm.1), custom_call_target="tpu_custom_call" | custom-call | flops 956301312 | bytes 2490368 | tf_op jit(solution)/shard_map/pallas_call | solution.py:287
  38.8 0.0 copy-done
  38.8 2.1 %shard_map.29 = bf16[152,8192]{1,0:T(8,128)(2,1)} custom-call(f32[4,4,4,152,128]{4,3,2,1,0:T(8,128)S(1)} %shard_map.28.work_ref, bf16[152,8192]{1,0:T(8,128)(2,1)S(1)} %copy-done), custom_call_target="tpu_custom_call" | custom-call | flops 7471104 | bytes 4980736 | tf_op jit(solution)/shard_map/pallas_call | solution.py:311
Async XLA Ops:
  0.0 38.8 %copy-start = (bf16[152,8192]{1,0:T(8,128)(2,1)S(1)}, bf16[152,8192]{1,0:T(8,128)(2,1)}, u32[]{:S(2)}) copy-start(bf16[152,8192]{1,0:T(8,128)(2,1)} %resident.1) | copy-start | bytes 7471108

commit v3 on v2

--- a/solution.py
+++ b/solution.py
@@ -14,10 +14,13 @@
 FAR_A = ((2, 0), (3, 1))
 FAR_B = ((0, 1), (3, 2))
 ARRIVALS = (
-    (0, 0), (1, 0), (3, 0), (2, 0), (0, 2), (1, 1), (3, 1), (3, 2),
-    (1, 2), (1, 3), (3, 3), (2, 2), (2, 3), (2, 1), (0, 1), (0, 3),
+    (0, 0), (1, 0), (3, 0), (2, 0), (0, 1), (0, 3), (1, 1), (1, 3),
+    (3, 1), (3, 3), (0, 2), (3, 2), (2, 1), (2, 3), (1, 2), (2, 2),
 )
+
 MESH = pl.DeviceIdType.MESH
+
+
 def window_of(feats):
     return -(-(CORES * feats + LANES - 1) // LANES) * LANES
 
@@ -135,10 +138,11 @@
         da, db = (step, 0) if way < 2 else (0, step)
         send(src, relay.at[way, slot], relay_sems.at[way, slot], device_at(da, db, core))
 
-    def to_end(src, step, da, db):
-        source = device_at(SIDE - da, db, core)
+    def to_ends(blocks):
         for c in range(CORES):
-            send(src.at[c], received.at[source], recv_sems.at[source], device_at(0, step, c))
+            for src, step, da, db in blocks:
+                source = device_at(SIDE - da, db, core)
+                send(src.at[c], received.at[source], recv_sems.at[source], device_at(0, step, c))
 
     def far_a(slot):
         for way in range(2):
@@ -150,22 +154,26 @@
         for da in (1, 3):
             to_middle(sending.at[da, db], da, da, db)
 
-    def far_b(way, slot):
-        da = FAR_B[way - 2][slot]
-        wait_held(da, 2)
-        to_relay(held(da, 2), way, slot)
-
-    def near_b(da, db):
-        wait_held(da, db)
-        to_end(held(da, db), db, da, 0)
-
-    def hand_on(way, slot):
-        wait(relay.at[way, slot], relay_sems.at[way, slot])
-        step = (1, 3)[way % 2]
-        if way < 2:
-            to_middle(relay.at[way, slot], step, 2, FAR_A[way][slot])
-        else:
-            to_end(relay.at[way, slot], step, FAR_B[way - 2][slot], SIDE - step)
+    def far_b(slot):
+        for way in (2, 3):
+            wait_held(FAR_B[way - 2][slot], 2)
+        for way in (2, 3):
+            to_relay(held(FAR_B[way - 2][slot], 2), way, slot)
+
+    def near_b(da):
+        for db in (1, 3):
+            wait_held(da, db)
+        to_ends([(held(da, db), db, da, 0) for db in (1, 3)])
+
+    def on_a(slot):
+        for way in range(2):
+            wait(relay.at[way, slot], relay_sems.at[way, slot])
+            to_middle(relay.at[way, slot], (1, 3)[way], 2, FAR_A[way][slot])
+
+    def on_b(slot):
+        for way in (2, 3):
+            wait(relay.at[way, slot], relay_sems.at[way, slot])
+        to_ends([(relay.at[way, slot], step, FAR_B[way - 2][slot], SIDE - step) for way, step in ((2, 1), (3, 3))])
 
     def home(da):
         wait_held(da, 0)
@@ -181,39 +189,31 @@
 
     far_a(0)
     load.wait()
-    make(0, 2)
-    far_b(2, 0)
-    near_a(2)
     for way in range(2):
         make(2, FAR_A[way][1])
     far_a(1)
-    hand_on(0, 0)
-    hand_on(1, 0)
+    near_a(2)
     near_a(1)
-    far_b(3, 0)
-    far_b(2, 1)
+    on_a(0)
     near_a(3)
-    hand_on(0, 1)
-    hand_on(1, 1)
-    far_b(3, 1)
-    hand_on(2, 0)
+    on_a(1)
     near_a(0)
-    near_b(1, 1)
-    near_b(3, 1)
-    hand_on(3, 0)
-    hand_on(2, 1)
-    near_b(1, 3)
-    near_b(3, 3)
-    hand_on(3, 1)
-    near_b(2, 3)
-    near_b(2, 1)
+
+    make(0, 2)
+    far_b(0)
     make(0, 1)
     make(0, 3)
-    near_b(0, 1)
-    near_b(0, 3)
+    near_b(0)
+    far_b(1)
+    near_b(1)
+    near_b(3)
     make(0, 0)
-    for da in (0, 1, 3, 2):
+    home(0)
+    on_b(0)
+    near_b(2)
+    for da in (1, 3, 2):
         home(da)
+    on_b(1)
 
     matrix = sylvester(LANES)
 

time: 41 us -> 39.5 us (0.963)
  Pallas kernels: 40.9 us -> 39.4 us
    pallas_call x1, Pallas kernels: 38.8 us -> 37.3 us  [shards(): pl.pallas_call(exchange_kernel, out_shape=pltpu.VMEM((SIDE, SIDE, 2 * COR...]
where the time goes in v3:
time: 39.5 us
  Pallas kernels  39.4 us (100%)
    pallas_call x1, Pallas kernels, shards(): pl.pallas_call(exchange_kernel, out_shape=pltpu.VMEM((SIDE, SIDE, 2 * COR...  37.3 us
    pallas_call x1, Pallas kernels, shards(): pl.pallas_call(finish_kernel, out_shape=jax.ShapeDtypeStruct(resident.sha...  2.14 us

profile of v3, /device:TPU:1, one launch (start us, length us, event | category | flops | bytes accessed | tf_op | source)
XLA Modules:
  0.0 39.5 jit_solution(13112167676169198447)
XLA Ops:
  0.0 0.0 copy-start
  0.0 37.3 %shard_map.28.work_ref = f32[4,4,4,152,128]{4,3,2,1,0:T(8,128)S(1)} custom-call(bf16[256,4864]{1,0:T(8,128)(2,1)} %update_hbm.1), custom_call_target="tpu_custom_call" | custom-call | flops 956301312 | bytes 2490368 | tf_op jit(solution)/shard_map/pallas_call | solution.py:287
  37.3 0.0 copy-done
  37.3 2.1 %shard_map.29 = bf16[152,8192]{1,0:T(8,128)(2,1)} custom-call(f32[4,4,4,152,128]{4,3,2,1,0:T(8,128)S(1)} %shard_map.28.work_ref, bf16[152,8192]{1,0:T(8,128)(2,1)S(1)} %copy-done), custom_call_target="tpu_custom_call" | custom-call | flops 7471104 | bytes 4980736 | tf_op jit(solution)/shard_map/pallas_call | solution.py:311
Async XLA Ops:
  0.0 37.3 %copy-start = (bf16[152,8192]{1,0:T(8,128)(2,1)S(1)}, bf16[152,8192]{1,0:T(8,128)(2,1)}, u32[]{:S(2)}) copy-start(bf16[152,8192]{1,0:T(8,128)(2,1)} %resident.1) | copy-start | bytes 7471108

commit v4 on v3

--- a/solution.py
+++ b/solution.py
@@ -13,12 +13,20 @@
 CHUNK = 16
 FAR_A = ((2, 0), (3, 1))
 FAR_B = ((0, 1), (3, 2))
+PAIRS = (
+    ((2, 2), (2, 3)), ((2, 0), (2, 1)), ((1, 2), (3, 2)), ((1, 1), (3, 1)),
+    ((1, 3), (3, 3)), ((1, 0), (3, 0)), ((0, 2), (0, 1)), ((0, 3), (0, 0)),
+)
 ARRIVALS = (
-    (0, 0), (1, 0), (3, 0), (2, 0), (0, 1), (0, 3), (1, 1), (1, 3),
-    (3, 1), (3, 3), (0, 2), (3, 2), (2, 1), (2, 3), (1, 2), (2, 2),
+    (0, 0), (1, 0), (0, 1), (3, 0), (0, 3), (1, 1),
+    (3, 3), (1, 3), (3, 1), (2, 0), (0, 2), (2, 3),
 )
-
+LAST = (((3, 2),), ((2, 1), (1, 2), (2, 2)))
 MESH = pl.DeviceIdType.MESH
+
+
+def numbers(rows):
+    return tuple(sum(row[at] * SIDE**place for place, row in enumerate(rows)) for at in range(len(rows[0])))
 
 
 def window_of(feats):
@@ -29,7 +37,7 @@
     rows = lax.broadcasted_iota(jnp.int32, (order, order), 0)
     cols = lax.broadcasted_iota(jnp.int32, (order, order), 1)
     parity = rows & cols
-    for shift in (4, 2, 1):
+    for shift in (8, 4, 2, 1):
         parity = parity ^ (parity >> shift)
     return (1 - 2 * (parity & 1)).astype(jnp.float32).astype(jnp.bfloat16)
 
@@ -83,7 +91,7 @@
         return pl.ds(pl.multiple_of(first * LANES, LANES), window), chip * CORES * feats - first * LANES
 
     firsts = [
-        pltpu.make_async_copy(update_hbm.at[:, window_at(2, FAR_A[way][0])[0]], early.at[way], early_sems.at[way])
+        pltpu.make_async_copy(update_hbm.at[:, window_at(*PAIRS[0][way])[0]], early.at[way], early_sems.at[way])
         for way in range(2)
     ]
     load = pltpu.make_async_copy(update_hbm, update, load_sem)
@@ -110,12 +118,11 @@
     sends = []
 
     def send(src, dst, sem, device):
-        copy = pltpu.make_async_remote_copy(
+        pltpu.make_async_remote_copy(
             src_ref=src, dst_ref=dst, send_sem=send_sems.at[len(sends)], recv_sem=sem,
             device_id={"inp": device}, device_id_type=MESH,
-        )
-        copy.start()
-        sends.append(copy)
+        ).start()
+        sends.append(len(src.shape))
 
     def wait(dst, sem):
         pltpu.make_async_remote_copy(
@@ -149,8 +156,6 @@
             to_relay(sending.at[2, FAR_A[way][slot]], way, slot)
 
     def near_a(db):
-        for da in (1, 3):
-            make(da, db)
         for da in (1, 3):
             to_middle(sending.at[da, db], da, da, db)
 
@@ -184,30 +189,44 @@
 
     for way in range(2):
         firsts[way].wait()
-        make(2, FAR_A[way][0], early[way])
+    for way in range(2):
+        make(*PAIRS[0][way], early[way])
     pl.semaphore_wait(barrier, len(others))
-
     far_a(0)
     load.wait()
-    for way in range(2):
-        make(2, FAR_A[way][1])
-    far_a(1)
-    near_a(2)
-    near_a(1)
-    on_a(0)
-    near_a(3)
-    on_a(1)
-    near_a(0)
-
-    make(0, 2)
-    far_b(0)
-    make(0, 1)
-    make(0, 3)
+
+    def second():
+        far_a(1)
+
+    def third():
+        near_a(2)
+
+    def fourth():
+        near_a(1)
+        on_a(0)
+
+    def fifth():
+        near_a(3)
+        on_a(1)
+
+    def sixth():
+        near_a(0)
+
+    def seventh():
+        far_b(0)
+
+    def make_pair(pair, digits):
+        for at in range(2):
+            make(digits[2 * at] % SIDE, digits[2 * at + 1] % SIDE)
+        for at, action in enumerate((second, third, fourth, fifth, sixth, seventh)):
+            pl.when(pair == at)(action)
+        return tuple(digit // SIDE for digit in digits)
+
+    lax.fori_loop(0, len(PAIRS) - 1, make_pair, numbers([one + other for one, other in PAIRS[1:]]))
     near_b(0)
     far_b(1)
     near_b(1)
     near_b(3)
-    make(0, 0)
     home(0)
     on_b(0)
     near_b(2)
@@ -215,35 +234,43 @@
         home(da)
     on_b(1)
 
-    matrix = sylvester(LANES)
-
-    def rotate(da, db, c):
-        x, y = (da, db)[c], (db, da)[c]
-        from_x, from_y = (my_x + SIDE - x) % SIDE, (my_y + SIDE - y) % SIDE
-        source = (from_y * SIDE + from_x) * CORES + c
-        if db == 0:
-            @pl.when(core != c)
-            def _():
-                wait(received.at[source], recv_sems.at[source])
-        else:
-            wait(received.at[source], recv_sems.at[source])
-        both = jnp.dot(received[source], matrix, preferred_element_type=jnp.float32)
-        halves = both[:feats] + both[feats:], both[:feats] - both[feats:]
-        if ARRIVALS.index((da, db)) < ARRIVALS.index((db, da)) or (da == db and c == 0):
-            for half in range(2):
-                work_ref[from_y, from_x, 2 * c + half] = halves[half]
-        else:
-            for half in range(2):
-                there = work_ref[from_y, from_x, 2 * (1 - c) + half]
-                work_ref[from_y, from_x, half] = halves[half] + there
-                work_ref[from_y, from_x, 2 + half] = halves[half] - there if c == 0 else there - halves[half]
-
-    for da, db in ARRIVALS:
-        for c in range(CORES):
-            rotate(da, db, c)
-
-    for copy in sends:
-        copy.wait_send()
+    matrix = sylvester(2 * LANES)
+
+    def rotate(*chips):
+        places = []
+        for x, y in chips:
+            places.append(((my_x + SIDE - x) % SIDE, (my_y + SIDE - y) % SIDE))
+            first = (places[-1][1] * SIDE + places[-1][0]) * CORES
+            for c, other in enumerate((y + core, x + 1 - core)):
+
+                @pl.when(other > 0)
+                def _(source=first + c):
+                    wait(received.at[source], recv_sems.at[source])
+
+        for from_x, from_y in places:
+            first = (from_y * SIDE + from_x) * CORES
+            pair = jnp.concatenate([received[first], received[first + 1]], axis=1)
+            both = jnp.dot(pair, matrix, preferred_element_type=jnp.float32)
+            low, high = both[:feats], both[feats:]
+            for half, value in enumerate((low + high, low - high)):
+                for c in range(CORES):
+                    work_ref[from_y, from_x, 2 * c + half] = value[:, c * LANES : (c + 1) * LANES]
+
+    def rotate_pair(_, digits):
+        rotate(*((digits[2 * at] % SIDE, digits[2 * at + 1] % SIDE) for at in range(2)))
+        return tuple(digit // SIDE for digit in digits)
+
+    pairs = [one + other for one, other in zip(ARRIVALS[::2], ARRIVALS[1::2])]
+    lax.fori_loop(0, len(pairs), rotate_pair, numbers(pairs))
+    for chips in LAST:
+        rotate(*chips)
+
+    for at, dims in enumerate(sends):
+        src = received.at[0] if dims == 2 else sending.at[0, 0]
+        pltpu.make_async_remote_copy(
+            src_ref=src, dst_ref=src, send_sem=send_sems.at[at], recv_sem=send_sems.at[at],
+            device_id={"inp": me}, device_id_type=MESH,
+        ).wait_send()
 
 
 def finish_kernel(work_ref, resident, out_hbm, out, out_sems):

time: 39.5 us -> 38.6 us (0.977)
  Pallas kernels: 39.4 us -> 38.5 us
    pallas_call x1, Pallas kernels: 37.3 us -> 36.3 us  [shards(): pl.pallas_call(exchange_kernel, out_shape=pltpu.VMEM((SIDE, SIDE, 2 * COR...]
where the time goes in v4:
time: 38.6 us; the launch traced here: 38.5 us
  Pallas kernels  38.5 us (100%)
    pallas_call x1, Pallas kernels, shards(): pl.pallas_call(exchange_kernel, out_shape=pltpu.VMEM((SIDE, SIDE, 2 * COR...  36.3 us
    pallas_call x1, Pallas kernels, shards(): pl.pallas_call(finish_kernel, out_shape=jax.ShapeDtypeStruct(resident.sha...  2.14 us

profile of v4, /device:TPU:1, one launch (start us, length us, event | category | flops | bytes accessed | tf_op | source)
XLA Modules:
  0.0 38.5 jit_solution(5518921941766785943)
XLA Ops:
  0.0 0.0 copy-start
  0.0 36.3 %shard_map.28.work_ref = f32[4,4,4,152,128]{4,3,2,1,0:T(8,128)S(1)} custom-call(bf16[256,4864]{1,0:T(8,128)(2,1)} %update_hbm.1), custom_call_target="tpu_custom_call" | custom-call | flops 956301312 | bytes 2490368 | tf_op jit(solution)/shard_map/pallas_call | solution.py:314
  36.3 0.0 copy-done
  36.3 2.1 %shard_map.29 = bf16[152,8192]{1,0:T(8,128)(2,1)} custom-call(f32[4,4,4,152,128]{4,3,2,1,0:T(8,128)S(1)} %shard_map.28.work_ref, bf16[152,8192]{1,0:T(8,128)(2,1)S(1)} %copy-done), custom_call_target="tpu_custom_call" | custom-call | flops 7471104 | bytes 4980736 | tf_op jit(solution)/shard_map/pallas_call | solution.py:338
Async XLA Ops:
  0.0 36.3 %copy-start = (bf16[152,8192]{1,0:T(8,128)(2,1)S(1)}, bf16[152,8192]{1,0:T(8,128)(2,1)}, u32[]{:S(2)}) copy-start(bf16[152,8192]{1,0:T(8,128)(2,1)} %resident.1) | copy-start | bytes 7471108

commit v5 on v4

--- a/solution.py
+++ b/solution.py
@@ -19,9 +19,9 @@
 )
 ARRIVALS = (
     (0, 0), (1, 0), (0, 1), (3, 0), (0, 3), (1, 1),
-    (3, 3), (1, 3), (3, 1), (2, 0), (0, 2), (2, 3),
+    (2, 0), (0, 2), (2, 3), (3, 2), (2, 1), (1, 2),
 )
-LAST = (((3, 2),), ((2, 1), (1, 2), (2, 2)))
+LAST = (((2, 2),), ((3, 1), (1, 3), (3, 3)))
 MESH = pl.DeviceIdType.MESH
 
 
@@ -226,13 +226,12 @@
     near_b(0)
     far_b(1)
     near_b(1)
+    near_b(2)
+    on_b(0)
+    on_b(1)
     near_b(3)
-    home(0)
-    on_b(0)
-    near_b(2)
-    for da in (1, 3, 2):
+    for da in (0, 1, 3, 2):
         home(da)
-    on_b(1)
 
     matrix = sylvester(2 * LANES)
 

time: 38.6 us -> 38.6 us (level)
  no operation moved by 1% of the time
where the time goes in v5:
time: 38.6 us; the launch traced here: 38.5 us
  Pallas kernels  38.5 us (100%)
    pallas_call x1, Pallas kernels, shards(): pl.pallas_call(exchange_kernel, out_shape=pltpu.VMEM((SIDE, SIDE, 2 * COR...  36.3 us
    pallas_call x1, Pallas kernels, shards(): pl.pallas_call(finish_kernel, out_shape=jax.ShapeDtypeStruct(resident.sha...  2.14 us

profile of v5, /device:TPU:1, one launch (start us, length us, event | category | flops | bytes accessed | tf_op | source)
XLA Modules:
  0.0 38.5 jit_solution(1812540310249131854)
XLA Ops:
  0.0 0.0 copy-start
  0.0 36.3 %shard_map.28.work_ref = f32[4,4,4,152,128]{4,3,2,1,0:T(8,128)S(1)} custom-call(bf16[256,4864]{1,0:T(8,128)(2,1)} %update_hbm.1), custom_call_target="tpu_custom_call" | custom-call | flops 956301312 | bytes 2490368 | tf_op jit(solution)/shard_map/pallas_call | solution.py:313
  36.3 0.0 copy-done
  36.3 2.1 %shard_map.29 = bf16[152,8192]{1,0:T(8,128)(2,1)} custom-call(f32[4,4,4,152,128]{4,3,2,1,0:T(8,128)S(1)} %shard_map.28.work_ref, bf16[152,8192]{1,0:T(8,128)(2,1)S(1)} %copy-done), custom_call_target="tpu_custom_call" | custom-call | flops 7471104 | bytes 4980736 | tf_op jit(solution)/shard_map/pallas_call | solution.py:337
Async XLA Ops:
  0.0 36.3 %copy-start = (bf16[152,8192]{1,0:T(8,128)(2,1)S(1)}, bf16[152,8192]{1,0:T(8,128)(2,1)}, u32[]{:S(2)}) copy-start(bf16[152,8192]{1,0:T(8,128)(2,1)} %resident.1) | copy-start | bytes 7471108

commit v6 on v4

--- a/solution.py
+++ b/solution.py
@@ -42,10 +42,10 @@
     return (1 - 2 * (parity & 1)).astype(jnp.float32).astype(jnp.bfloat16)
 
 
-def selection(order, window, shift):
-    rows = lax.broadcasted_iota(jnp.int32, (order, window), 0)
-    cols = lax.broadcasted_iota(jnp.int32, (order, window), 1)
-    return jnp.where(cols == rows + shift, 1.0, 0.0).astype(jnp.bfloat16)
+def identity(order):
+    rows = lax.broadcasted_iota(jnp.int32, (order, order), 0)
+    cols = lax.broadcasted_iota(jnp.int32, (order, order), 1)
+    return jnp.where(rows == cols, 1.0, 0.0).astype(jnp.bfloat16)
 
 
 def butterfly(values):
@@ -61,7 +61,7 @@
 
 
 def exchange_kernel(
-    update_hbm, work_ref, update, early, sending, middle, relay, received,
+    update_hbm, work_ref, update, early, eye, sending, middle, relay, received,
     load_sem, early_sems, send_sems, middle_sems, relay_sems, recv_sems,
 ):
     cols = update.shape[1]
@@ -106,7 +106,7 @@
     def make(da, db, columns=None):
         at, shift = window_at(da, db)
         turned = lax.dot_general(
-            selection(CORES * feats, window, shift),
+            eye[pl.ds(pl.multiple_of(shift, 16), CORES * feats), :],
             update[:, at] if columns is None else columns,
             (((1,), (1,)), ((), ())),
             preferred_element_type=jnp.float32,
@@ -187,6 +187,7 @@
         send(block.at[1 - core], received.at[source], recv_sems.at[source], device_at(0, 0, 1 - core))
         received[source] = block[core]
 
+    eye[...] = identity(window)
     for way in range(2):
         firsts[way].wait()
     for way in range(2):
@@ -235,6 +236,7 @@
     on_b(1)
 
     matrix = sylvester(2 * LANES)
+    factor = 1.0 / jnp.sqrt(jnp.float32(groups * 2 * LANES))
 
     def rotate(*chips):
         places = []
@@ -254,7 +256,7 @@
             low, high = both[:feats], both[feats:]
             for half, value in enumerate((low + high, low - high)):
                 for c in range(CORES):
-                    work_ref[from_y, from_x, 2 * c + half] = value[:, c * LANES : (c + 1) * LANES]
+                    work_ref[from_y, from_x, 2 * c + half] = value[:, c * LANES : (c + 1) * LANES] * factor
 
     def rotate_pair(_, digits):
         rotate(*((digits[2 * at] % SIDE, digits[2 * at + 1] % SIDE) for at in range(2)))
@@ -275,7 +277,6 @@
 
 def finish_kernel(work_ref, resident, out_hbm, out, out_sems):
     feats, width = out.shape
-    factor = 1.0 / jnp.sqrt(jnp.float32(width))
     whole = feats // CHUNK
 
     def store(chunk, rows):
@@ -286,7 +287,7 @@
             values = butterfly([work_ref[y, x, at, rows, :] for y in range(SIDE) for x in range(SIDE)])
             for chip, value in enumerate(values):
                 cols = pl.ds((chip * 2 * CORES + at) * LANES, LANES)
-                total = resident[rows, cols].astype(jnp.float32) + value * factor
+                total = resident[rows, cols].astype(jnp.float32) + value
                 out[rows, cols] = total.astype(out.dtype)
 
     @pl.loop(0, whole)
@@ -319,6 +320,7 @@
         scratch_shapes=[
             pltpu.VMEM((rows, cols), weight_delta.dtype),
             pltpu.VMEM((2, rows, window_of(feats)), weight_delta.dtype),
+            pltpu.VMEM((window_of(feats), window_of(feats)), weight_delta.dtype),
             pltpu.VMEM((SIDE, SIDE, CORES, 2 * feats, LANES), weight_delta.dtype),
             pltpu.VMEM((SIDE, SIDE, CORES, 2 * feats, LANES), weight_delta.dtype),
             pltpu.VMEM((4, 2, CORES, 2 * feats, LANES), weight_delta.dtype),

time: 38.6 us -> 38.4 us (level)
  no operation moved by 1% of the time
where the time goes in v6:
time: 38.4 us; the launch traced here: 38.3 us
  Pallas kernels  38.3 us (100%)
    pallas_call x1, Pallas kernels, shards(): pl.pallas_call(exchange_kernel, out_shape=pltpu.VMEM((SIDE, SIDE, 2 * COR...  36.3 us
    pallas_call x1, Pallas kernels, shards(): pl.pallas_call(finish_kernel, out_shape=jax.ShapeDtypeStruct(resident.sha...  1.99 us

profile of v6, /device:TPU:1, one launch (start us, length us, event | category | flops | bytes accessed | tf_op | source)
XLA Modules:
  0.0 38.3 jit_solution(422022308021327686)
XLA Ops:
  0.0 0.0 copy-start
  0.0 36.3 %shard_map.28.work_ref = f32[4,4,4,152,128]{4,3,2,1,0:T(8,128)S(1)} custom-call(bf16[256,4864]{1,0:T(8,128)(2,1)} %update_hbm.1), custom_call_target="tpu_custom_call" | custom-call | flops 956301312 | bytes 2490368 | tf_op jit(solution)/shard_map/pallas_call | solution.py:315
  36.3 0.0 copy-done
  36.4 2.0 %shard_map.29 = bf16[152,8192]{1,0:T(8,128)(2,1)} custom-call(f32[4,4,4,152,128]{4,3,2,1,0:T(8,128)S(1)} %shard_map.28.work_ref, bf16[152,8192]{1,0:T(8,128)(2,1)S(1)} %copy-done), custom_call_target="tpu_custom_call" | custom-call | flops 7471104 | bytes 4980736 | tf_op jit(solution)/shard_map/pallas_call | solution.py:340
Async XLA Ops:
  0.0 36.3 %copy-start = (bf16[152,8192]{1,0:T(8,128)(2,1)S(1)}, bf16[152,8192]{1,0:T(8,128)(2,1)}, u32[]{:S(2)}) copy-start(bf16[152,8192]{1,0:T(8,128)(2,1)} %resident.1) | copy-start | bytes 7471108

commit v7 on v6

--- a/solution.py
+++ b/solution.py
@@ -22,6 +22,7 @@
     (3, 3), (1, 3), (3, 1), (2, 0), (0, 2), (2, 3),
 )
 LAST = (((3, 2),), ((2, 1), (1, 2), (2, 2)))
+ALONG_A, ALONG_B, HOME = range(3)
 MESH = pl.DeviceIdType.MESH
 
 
@@ -115,14 +116,11 @@
             rows = turned[c * feats : (c + 1) * feats]
             sending[da, db, c] = jnp.concatenate([rows[:, :LANES], rows[:, LANES:]], axis=0).astype(sending.dtype)
 
-    sends = []
-
-    def send(src, dst, sem, device):
+    def send(src, dst, kind, sem, device):
         pltpu.make_async_remote_copy(
-            src_ref=src, dst_ref=dst, send_sem=send_sems.at[len(sends)], recv_sem=sem,
+            src_ref=src, dst_ref=dst, send_sem=send_sems.at[kind], recv_sem=sem,
             device_id={"inp": device}, device_id_type=MESH,
         ).start()
-        sends.append(len(src.shape))
 
     def wait(dst, sem):
         pltpu.make_async_remote_copy(
@@ -138,18 +136,18 @@
             wait(middle.at[da, db], middle_sems.at[da, db])
 
     def to_middle(src, step, da, db):
-        send(src, middle.at[da, db], middle_sems.at[da, db], device_at(step, 0, core))
+        send(src, middle.at[da, db], ALONG_A, middle_sems.at[da, db], device_at(step, 0, core))
 
     def to_relay(src, way, slot):
         step = (1, 3)[way % 2]
         da, db = (step, 0) if way < 2 else (0, step)
-        send(src, relay.at[way, slot], relay_sems.at[way, slot], device_at(da, db, core))
+        send(src, relay.at[way, slot], way // 2, relay_sems.at[way, slot], device_at(da, db, core))
 
     def to_ends(blocks):
         for c in range(CORES):
             for src, step, da, db in blocks:
                 source = device_at(SIDE - da, db, core)
-                send(src.at[c], received.at[source], recv_sems.at[source], device_at(0, step, c))
+                send(src.at[c], received.at[source], ALONG_B, recv_sems.at[source], device_at(0, step, c))
 
     def far_a(slot):
         for way in range(2):
@@ -184,7 +182,7 @@
         wait_held(da, 0)
         block = held(da, 0)
         source = device_at(SIDE - da, 0, core)
-        send(block.at[1 - core], received.at[source], recv_sems.at[source], device_at(0, 0, 1 - core))
+        send(block.at[1 - core], received.at[source], HOME, recv_sems.at[source], device_at(0, 0, 1 - core))
         received[source] = block[core]
 
     eye[...] = identity(window)
@@ -267,10 +265,9 @@
     for chips in LAST:
         rotate(*chips)
 
-    for at, dims in enumerate(sends):
-        src = received.at[0] if dims == 2 else sending.at[0, 0]
+    for kind, sent in ((ALONG_A, sending), (ALONG_B, sending), (HOME, received.at[pl.ds(0, SIDE)])):
         pltpu.make_async_remote_copy(
-            src_ref=src, dst_ref=src, send_sem=send_sems.at[at], recv_sem=send_sems.at[at],
+            src_ref=sent, dst_ref=sent, send_sem=send_sems.at[kind], recv_sem=send_sems.at[kind],
             device_id={"inp": me}, device_id_type=MESH,
         ).wait_send()
 
@@ -327,7 +324,7 @@
             pltpu.VMEM((groups, 2 * feats, LANES), weight_delta.dtype),
             pltpu.SemaphoreType.DMA,
             pltpu.SemaphoreType.DMA((2,)),
-            pltpu.SemaphoreType.DMA((64,)),
+            pltpu.SemaphoreType.DMA((3,)),
             pltpu.SemaphoreType.DMA((SIDE, SIDE)),
             pltpu.SemaphoreType.DMA((4, 2)),
             pltpu.SemaphoreType.DMA((groups,)),

time: 38.4 us -> 37.8 us (0.984)
  Pallas kernels: 38.3 us -> 37.7 us
    pallas_call x1, Pallas kernels: 36.3 us -> 35.7 us  [shards(): pl.pallas_call(exchange_kernel, out_shape=pltpu.VMEM((SIDE, SIDE, 2 * COR...]
where the time goes in v7:
time: 37.8 us; the launch traced here: 37.7 us
  Pallas kernels  37.7 us (100%)
    pallas_call x1, Pallas kernels, shards(): pl.pallas_call(exchange_kernel, out_shape=pltpu.VMEM((SIDE, SIDE, 2 * COR...  35.7 us
    pallas_call x1, Pallas kernels, shards(): pl.pallas_call(finish_kernel, out_shape=jax.ShapeDtypeStruct(resident.sha...  1.99 us

profile of v7, /device:TPU:1, one launch (start us, length us, event | category | flops | bytes accessed | tf_op | source)
XLA Modules:
  0.0 37.7 jit_solution(367582411958988563)
XLA Ops:
  0.0 0.0 copy-start
  0.0 35.7 %shard_map.28.work_ref = f32[4,4,4,152,128]{4,3,2,1,0:T(8,128)S(1)} custom-call(bf16[256,4864]{1,0:T(8,128)(2,1)} %update_hbm.1), custom_call_target="tpu_custom_call" | custom-call | flops 956301312 | bytes 2490368 | tf_op jit(solution)/shard_map/pallas_call | solution.py:312
  35.7 0.0 copy-done
  35.7 2.0 %shard_map.29 = bf16[152,8192]{1,0:T(8,128)(2,1)} custom-call(f32[4,4,4,152,128]{4,3,2,1,0:T(8,128)S(1)} %shard_map.28.work_ref, bf16[152,8192]{1,0:T(8,128)(2,1)S(1)} %copy-done), custom_call_target="tpu_custom_call" | custom-call | flops 7471104 | bytes 4980736 | tf_op jit(solution)/shard_map/pallas_call | solution.py:337
Async XLA Ops:
  0.0 35.7 %copy-start = (bf16[152,8192]{1,0:T(8,128)(2,1)S(1)}, bf16[152,8192]{1,0:T(8,128)(2,1)}, u32[]{:S(2)}) copy-start(bf16[152,8192]{1,0:T(8,128)(2,1)} %resident.1) | copy-start | bytes 7471108

commit v8 on v7

--- a/solution.py
+++ b/solution.py
@@ -79,12 +79,14 @@
     my_b = my_y + core * (my_x - my_y)
 
     def chip_at(da, db):
-        a, b = (my_a + da) % SIDE, (my_b + db) % SIDE
+        a, b = lax.rem(my_a + da, SIDE), lax.rem(my_b + db, SIDE)
         x, y = a + core * (b - a), b + core * (a - b)
         return y * SIDE + x
 
+    firsts_of_chips = [[chip_at(da, db) * CORES for db in range(SIDE)] for da in range(SIDE)]
+
     def device_at(da, db, c):
-        return chip_at(da, db) * CORES + c
+        return firsts_of_chips[da % SIDE][db % SIDE] + c
 
     def window_at(da, db):
         chip = chip_at(da, db)
@@ -128,6 +130,12 @@
             device_id={"inp": me}, device_id_type=MESH,
         ).wait_recv()
 
+    def wait_sent(kind, sent):
+        pltpu.make_async_remote_copy(
+            src_ref=sent, dst_ref=sent, send_sem=send_sems.at[kind], recv_sem=send_sems.at[kind],
+            device_id={"inp": me}, device_id_type=MESH,
+        ).wait_send()
+
     def held(da, db):
         return sending.at[da, db] if da == 0 else middle.at[da, db]
 
@@ -239,7 +247,7 @@
     def rotate(*chips):
         places = []
         for x, y in chips:
-            places.append(((my_x + SIDE - x) % SIDE, (my_y + SIDE - y) % SIDE))
+            places.append((lax.rem(my_x + SIDE - x, SIDE), lax.rem(my_y + SIDE - y, SIDE)))
             first = (places[-1][1] * SIDE + places[-1][0]) * CORES
             for c, other in enumerate((y + core, x + 1 - core)):
 
@@ -262,14 +270,11 @@
 
     pairs = [one + other for one, other in zip(ARRIVALS[::2], ARRIVALS[1::2])]
     lax.fori_loop(0, len(pairs), rotate_pair, numbers(pairs))
+    wait_sent(ALONG_A, sending)
+    wait_sent(HOME, received.at[pl.ds(0, SIDE)])
     for chips in LAST:
         rotate(*chips)
-
-    for kind, sent in ((ALONG_A, sending), (ALONG_B, sending), (HOME, received.at[pl.ds(0, SIDE)])):
-        pltpu.make_async_remote_copy(
-            src_ref=sent, dst_ref=sent, send_sem=send_sems.at[kind], recv_sem=send_sems.at[kind],
-            device_id={"inp": me}, device_id_type=MESH,
-        ).wait_send()
+    wait_sent(ALONG_B, sending)
 
 
 def finish_kernel(work_ref, resident, out_hbm, out, out_sems):

time: 37.8 us -> 37.8 us (level)
  no operation moved by 1% of the time
where the time goes in v8:
time: 37.8 us; the launch traced here: 37.7 us
  Pallas kernels  37.7 us (100%)
    pallas_call x1, Pallas kernels, shards(): pl.pallas_call(exchange_kernel, out_shape=pltpu.VMEM((SIDE, SIDE, 2 * COR...  35.7 us
    pallas_call x1, Pallas kernels, shards(): pl.pallas_call(finish_kernel, out_shape=jax.ShapeDtypeStruct(resident.sha...  1.99 us

profile of v8, /device:TPU:1, one launch (start us, length us, event | category | flops | bytes accessed | tf_op | source)
XLA Modules:
  0.0 37.7 jit_solution(7848652624265841677)
XLA Ops:
  0.0 0.0 copy-start
  0.0 35.7 %shard_map.28.work_ref = f32[4,4,4,152,128]{4,3,2,1,0:T(8,128)S(1)} custom-call(bf16[256,4864]{1,0:T(8,128)(2,1)} %update_hbm.1), custom_call_target="tpu_custom_call" | custom-call | flops 956301312 | bytes 2490368 | tf_op jit(solution)/shard_map/pallas_call | solution.py:317
  35.7 0.0 copy-done
  35.7 2.0 %shard_map.29 = bf16[152,8192]{1,0:T(8,128)(2,1)} custom-call(f32[4,4,4,152,128]{4,3,2,1,0:T(8,128)S(1)} %shard_map.28.work_ref, bf16[152,8192]{1,0:T(8,128)(2,1)S(1)} %copy-done), custom_call_target="tpu_custom_call" | custom-call | flops 7471104 | bytes 4980736 | tf_op jit(solution)/shard_map/pallas_call | solution.py:342
Async XLA Ops:
  0.0 35.7 %copy-start = (bf16[152,8192]{1,0:T(8,128)(2,1)S(1)}, bf16[152,8192]{1,0:T(8,128)(2,1)}, u32[]{:S(2)}) copy-start(bf16[152,8192]{1,0:T(8,128)(2,1)} %resident.1) | copy-start | bytes 7471108

commit v9 on v8

--- a/solution.py
+++ b/solution.py
@@ -277,36 +277,31 @@
     wait_sent(ALONG_B, sending)
 
 
-def finish_kernel(work_ref, resident, out_hbm, out, out_sems):
+def finish_kernel(work_ref, resident, out_hbm, out, out_sem):
     feats, width = out.shape
+    chips = SIDE * SIDE
     whole = feats // CHUNK
 
-    def store(chunk, rows):
-        return pltpu.make_async_copy(out.at[rows], out_hbm.at[rows], out_sems.at[chunk])
-
-    def finish(rows):
-        for at in range(2 * CORES):
+    def finish(core, rows):
+        for at in (2 * core, 2 * core + 1):
             values = butterfly([work_ref[y, x, at, rows, :] for y in range(SIDE) for x in range(SIDE)])
             for chip, value in enumerate(values):
                 cols = pl.ds((chip * 2 * CORES + at) * LANES, LANES)
                 total = resident[rows, cols].astype(jnp.float32) + value
                 out[rows, cols] = total.astype(out.dtype)
 
-    @pl.loop(0, whole)
-    def _(chunk):
-        rows = pl.ds(pl.multiple_of(chunk * CHUNK, CHUNK), CHUNK)
-        finish(rows)
-        store(chunk, rows).start()
-
-    rest = pl.ds(whole * CHUNK, feats % CHUNK)
-    if feats % CHUNK:
-        finish(rest)
-        store(whole, rest).start()
-        store(whole, rest).wait()
-
-    @pl.loop(0, whole)
-    def _(chunk):
-        store(chunk, pl.ds(pl.multiple_of(chunk * CHUNK, CHUNK), CHUNK)).wait()
+    for core in range(CORES):
+
+        @pl.loop(0, whole)
+        def _(chunk, core=core):
+            finish(core, pl.ds(pl.multiple_of(chunk * CHUNK, CHUNK), CHUNK))
+
+        if feats % CHUNK:
+            finish(core, pl.ds(whole * CHUNK, feats % CHUNK))
+        for chip in range(chips):
+            cols = pl.ds((chip * CORES + core) * 2 * LANES, 2 * LANES)
+            pltpu.make_async_copy(out.at[:, cols], out_hbm.at[:, cols], out_sem).start()
+    pltpu.make_async_copy(out, out_hbm, out_sem).wait()
 
 
 def shards(weight_delta, resident):
@@ -346,7 +341,7 @@
         out_specs=pl.BlockSpec(memory_space=pl.ANY),
         scratch_shapes=[
             pltpu.VMEM(resident.shape, resident.dtype),
-            pltpu.SemaphoreType.DMA((-(-feats // CHUNK),)),
+            pltpu.SemaphoreType.DMA,
         ],
         compiler_params=pltpu.CompilerParams(vmem_limit_bytes=32 * 1024 * 1024),
         cost_estimate=pl.CostEstimate(flops=6 * size, bytes_accessed=4 * size, transcendentals=0),

time: 37.8 us -> 38.1 us (level)
  no operation moved by 1% of the time
where the time goes in v9:
time: 38.1 us; the launch traced here: 38 us
  Pallas kernels  38 us (100%)
    pallas_call x1, Pallas kernels, shards(): pl.pallas_call(exchange_kernel, out_shape=pltpu.VMEM((SIDE, SIDE, 2 * COR...  35.7 us
    pallas_call x1, Pallas kernels, shards(): pl.pallas_call(finish_kernel, out_shape=jax.ShapeDtypeStruct(resident.sha...  2.32 us

profile of v9, /device:TPU:1, one launch (start us, length us, event | category | flops | bytes accessed | tf_op | source)
XLA Modules:
  0.0 38.0 jit_solution(13686720904605799178)
XLA Ops:
  0.0 0.0 copy-start
  0.0 35.7 %shard_map.28.work_ref = f32[4,4,4,152,128]{4,3,2,1,0:T(8,128)S(1)} custom-call(bf16[256,4864]{1,0:T(8,128)(2,1)} %update_hbm.1), custom_call_target="tpu_custom_call" | custom-call | flops 956301312 | bytes 2490368 | tf_op jit(solution)/shard_map/pallas_call | solution.py:312
  35.7 0.0 copy-done
  35.7 2.3 %shard_map.29 = bf16[152,8192]{1,0:T(8,128)(2,1)} custom-call(f32[4,4,4,152,128]{4,3,2,1,0:T(8,128)S(1)} %shard_map.28.work_ref, bf16[152,8192]{1,0:T(8,128)(2,1)S(1)} %copy-done), custom_call_target="tpu_custom_call" | custom-call | flops 7471104 | bytes 4980736 | tf_op jit(solution)/shard_map/pallas_call | solution.py:337
Async XLA Ops:
  0.0 35.7 %copy-start = (bf16[152,8192]{1,0:T(8,128)(2,1)S(1)}, bf16[152,8192]{1,0:T(8,128)(2,1)}, u32[]{:S(2)}) copy-start(bf16[152,8192]{1,0:T(8,128)(2,1)} %resident.1) | copy-start | bytes 7471108

commit v10 on v9

--- a/solution.py
+++ b/solution.py
@@ -282,24 +282,24 @@
     chips = SIDE * SIDE
     whole = feats // CHUNK
 
-    def finish(core, rows):
-        for at in (2 * core, 2 * core + 1):
+    def finish(group, rows):
+        for at in group:
             values = butterfly([work_ref[y, x, at, rows, :] for y in range(SIDE) for x in range(SIDE)])
             for chip, value in enumerate(values):
                 cols = pl.ds((chip * 2 * CORES + at) * LANES, LANES)
                 total = resident[rows, cols].astype(jnp.float32) + value
                 out[rows, cols] = total.astype(out.dtype)
 
-    for core in range(CORES):
+    for group in ((0, 1), (2,), (3,)):
 
         @pl.loop(0, whole)
-        def _(chunk, core=core):
-            finish(core, pl.ds(pl.multiple_of(chunk * CHUNK, CHUNK), CHUNK))
+        def _(chunk, group=group):
+            finish(group, pl.ds(pl.multiple_of(chunk * CHUNK, CHUNK), CHUNK))
 
         if feats % CHUNK:
-            finish(core, pl.ds(whole * CHUNK, feats % CHUNK))
+            finish(group, pl.ds(whole * CHUNK, feats % CHUNK))
         for chip in range(chips):
-            cols = pl.ds((chip * CORES + core) * 2 * LANES, 2 * LANES)
+            cols = pl.ds((chip * 2 * CORES + group[0]) * LANES, len(group) * LANES)
             pltpu.make_async_copy(out.at[:, cols], out_hbm.at[:, cols], out_sem).start()
     pltpu.make_async_copy(out, out_hbm, out_sem).wait()
 

time: 38.1 us -> 38 us (level)
  no operation moved by 1% of the time
where the time goes in v10:
time: 38 us; the launch traced here: 37.9 us
  Pallas kernels  37.9 us (100%)
    pallas_call x1, Pallas kernels, shards(): pl.pallas_call(exchange_kernel, out_shape=pltpu.VMEM((SIDE, SIDE, 2 * COR...  35.7 us
    pallas_call x1, Pallas kernels, shards(): pl.pallas_call(finish_kernel, out_shape=jax.ShapeDtypeStruct(resident.sha...  2.2 us

profile of v10, /device:TPU:1, one launch (start us, length us, event | category | flops | bytes accessed | tf_op | source)
XLA Modules:
  0.0 37.9 jit_solution(4023687506775950209)
XLA Ops:
  0.0 0.0 copy-start
  0.0 35.7 %shard_map.28.work_ref = f32[4,4,4,152,128]{4,3,2,1,0:T(8,128)S(1)} custom-call(bf16[256,4864]{1,0:T(8,128)(2,1)} %update_hbm.1), custom_call_target="tpu_custom_call" | custom-call | flops 956301312 | bytes 2490368 | tf_op jit(solution)/shard_map/pallas_call | solution.py:312
  35.7 0.0 copy-done
  35.7 2.2 %shard_map.29 = bf16[152,8192]{1,0:T(8,128)(2,1)} custom-call(f32[4,4,4,152,128]{4,3,2,1,0:T(8,128)S(1)} %shard_map.28.work_ref, bf16[152,8192]{1,0:T(8,128)(2,1)S(1)} %copy-done), custom_call_target="tpu_custom_call" | custom-call | flops 7471104 | bytes 4980736 | tf_op jit(solution)/shard_map/pallas_call | solution.py:337
Async XLA Ops:
  0.0 35.7 %copy-start = (bf16[152,8192]{1,0:T(8,128)(2,1)S(1)}, bf16[152,8192]{1,0:T(8,128)(2,1)}, u32[]{:S(2)}) copy-start(bf16[152,8192]{1,0:T(8,128)(2,1)} %resident.1) | copy-start | bytes 7471108
